TPU v7x, 32 devices: a whole 2x2x4 slice. The times are simulated.
32 devices in a mesh: dp: 4 (over z), ctx: 4 (over y, x), head: 2 (over core).
Axes of the slice: x: 2, y: 2, z: 4, core: 2. Of those that a mesh axis runs over, the one named last changes fastest.
Arguments:
- queries: bfloat16 [4, 1024, 12, 128], P('dp', 'ctx', 'head'), may hold values from -6 to 6
- keys: bfloat16 [4, 1024, 12, 128], P('dp', 'ctx', 'head'), may hold values from -0.5 to 0.5
- values: bfloat16 [4, 1024, 12, 128], P('dp', 'ctx', 'head'), may hold values from -6 to 6
- hidden_in: bfloat16 [4, 1024, 3072], P('dp', 'ctx'), may hold values from -6 to 6
- rate_weight: bfloat16 [12, 3072], P('head'), may hold values from -0.109375 to 0.109375
- state_init: float32 [12, 128, 128], P('head'), may hold values from -0.5 to 0.5
- out_grad: bfloat16 [4, 1024, 12, 128], P('dp', 'ctx', 'head'), may hold values from -6 to 6
Outputs:
- grad_queries: bfloat16 [4, 1024, 12, 128], P('dp', 'ctx', 'head')
- grad_keys: bfloat16 [4, 1024, 12, 128], P('dp', 'ctx', 'head')
- grad_values: bfloat16 [4, 1024, 12, 128], P('dp', 'ctx', 'head')
- grad_hidden: bfloat16 [4, 1024, 3072], P('dp', 'ctx')
- grad_rate_weight: float32 [12, 3072], P('head')
- grad_init: float32 [12, 128, 128], P('head')
All inputs are finite; a program needn't handle non-finite values.
Results may differ from a plain program's by a relative error of at most 0.0051.
Values may be sent and summed in bfloat16 or wider, within the bound.
A program may use at most 192 MiB of HBM per device.

v0:
```python
import jax
import jax.numpy as jnp
from jax import lax
from jax.sharding import PartitionSpec as P

MINI = 64


RATE_SCALE = 0.5


def prefix(value, axis, join, neutral, backward):
    count, mine = (lax.axis_size(axis), lax.axis_index(axis))
    pieces = jax.tree.map(lambda part: lax.all_gather(part, axis), value)
    if backward:
        pieces = jax.tree.map(lambda part: part[::-1], pieces)
        mine = count - 1 - mine
    subtotal = jax.tree.map(
        lambda part, zero: jnp.full_like(part, 0) + jnp.asarray(zero, part.dtype), value, neutral
    )

    def lap(position, subtotal):
        longer = join(subtotal, jax.tree.map(lambda part: part[position], pieces))
        return jax.tree.map(lambda new, old: jnp.where(position < mine, new, old), longer, subtotal)

    return lax.fori_loop(0, count - 1, lap, subtotal)


def product(left, right):
    return jnp.dot(left, right, precision=lax.Precision.HIGHEST, preferred_element_type=jnp.float32)


def stacked(left, right):
    return jnp.einsum(
        "...ij,...jk->...ik",
        left,
        right,
        precision=lax.Precision.HIGHEST,
        preferred_element_type=jnp.float32,
    )


def local_run(state, query_rows, key_rows, value_rows, logit_rows):
    rates = RATE_SCALE * jax.nn.sigmoid(logit_rows)
    block_count = query_rows.shape[0] // MINI
    width = query_rows.shape[1]

    def local_advance(current, block):
        query_block, key_block, value_block, rate_block = block
        residual = product(key_block, current) - value_block
        current = current - product(key_block.T, rate_block[:, None] * residual)
        return (current, product(query_block, current))

    blocks = (
        query_rows.reshape(block_count, MINI, width),
        key_rows.reshape(block_count, MINI, width),
        value_rows.reshape(block_count, MINI, width),
        rates.reshape(block_count, MINI),
    )
    final_state, layer_rows = lax.scan(local_advance, state, blocks)
    return (final_state, layer_rows.reshape(query_rows.shape))


def block_maps(key_rows, value_rows, logit_rows):
    rates = RATE_SCALE * jax.nn.sigmoid(logit_rows)
    block_count = key_rows.shape[0] // MINI
    width = key_rows.shape[1]

    def block_advance(carry, block):
        step_map, step_shift = carry
        key_block, value_block, rate_block = block
        key_gram = product(key_block.T, rate_block[:, None] * key_block)
        step_map = step_map - product(key_gram, step_map)
        step_shift = (
            step_shift
            - product(key_gram, step_shift)
            + product(key_block.T, rate_block[:, None] * value_block)
        )
        return ((step_map, step_shift), None)

    start = (jnp.eye(width, dtype=jnp.float32), jnp.zeros((width, width), jnp.float32))
    blocks = (
        key_rows.reshape(block_count, MINI, width),
        value_rows.reshape(block_count, MINI, width),
        rates.reshape(block_count, MINI),
    )
    result, unused = lax.scan(block_advance, start, blocks)
    return result


def compose(earlier, later):
    early_map, early_shift = earlier
    late_map, late_shift = later
    return (stacked(late_map, early_map), stacked(late_map, early_shift) + late_shift)


def local_term(query_rows, key_rows, value_rows, logit_rows, grad_rows):
    width = query_rows.shape[1]

    def only_state(state):
        return local_run(state, query_rows, key_rows, value_rows, logit_rows)

    unused, pullback = jax.vjp(only_state, jnp.zeros((width, width), jnp.float32))
    return pullback((jnp.zeros((width, width), jnp.float32), grad_rows))[0]


def full_grads(state, query_rows, key_rows, value_rows, logit_rows, later_grad, grad_rows):
    unused, pullback = jax.vjp(local_run, state, query_rows, key_rows, value_rows, logit_rows)
    return pullback((later_grad, grad_rows))


def arrange(array):
    return jnp.transpose(array.astype(jnp.float32), (0, 2, 1, 3))


def local(queries, keys, values, hidden_in, rate_weight, state_init, out_grad):
    seq_count, tok_count, head_count, head_width = queries.shape
    feat_count = hidden_in.shape[2]
    inputs_flat = hidden_in.reshape(seq_count * tok_count, feat_count)
    logits = jnp.dot(inputs_flat, rate_weight.T, preferred_element_type=jnp.float32)
    logit_rows = jnp.transpose(logits.reshape(seq_count, tok_count, head_count), (0, 2, 1))
    query_rows = arrange(queries)
    key_rows = arrange(keys)
    value_rows = arrange(values)
    grad_rows = arrange(out_grad)
    step_maps, step_shift = jax.vmap(jax.vmap(block_maps))(key_rows, value_rows, logit_rows)
    unit_maps = jnp.broadcast_to(jnp.eye(head_width, dtype=jnp.float32), step_maps.shape)
    zero_maps = jnp.zeros(step_maps.shape, jnp.float32)
    prefix_maps, prefix_shift = prefix(
        (step_maps, step_shift), "ctx", compose, (unit_maps, zero_maps), False
    )
    start_state = stacked(prefix_maps, state_init[None]) + prefix_shift
    local_terms = jax.vmap(jax.vmap(local_term))(
        query_rows, key_rows, value_rows, logit_rows, grad_rows
    )
    back_maps = jnp.swapaxes(step_maps, -1, -2)
    unused, later_grad = prefix(
        (back_maps, local_terms), "ctx", compose, (unit_maps, zero_maps), True
    )
    grad_state, grad_query, grad_key, grad_value, grad_logit = jax.vmap(jax.vmap(full_grads))(
        start_state, query_rows, key_rows, value_rows, logit_rows, later_grad, grad_rows
    )
    logit_flat = jnp.transpose(grad_logit, (0, 2, 1)).reshape(seq_count * tok_count, head_count)
    weight_term = jnp.dot(
        logit_flat.T,
        inputs_flat.astype(jnp.float32),
        precision=lax.Precision.HIGHEST,
        preferred_element_type=jnp.float32,
    )
    first_mask = (lax.axis_index("ctx") == 0).astype(jnp.float32)
    init_term = jnp.sum(grad_state, axis=0) * first_mask
    grad_init, grad_rate_weight = lax.psum((init_term, weight_term), ("dp", "ctx"))
    partial_hidden = product(logit_flat, rate_weight.astype(jnp.float32))
    grad_flat = lax.psum(partial_hidden.astype(jnp.bfloat16), "head")
    grad_hidden = grad_flat.reshape(seq_count, tok_count, feat_count)

    def back(array):
        return jnp.transpose(array, (0, 2, 1, 3)).astype(jnp.bfloat16)

    return (
        back(grad_query),
        back(grad_key),
        back(grad_value),
        grad_hidden,
        grad_rate_weight,
        grad_init,
    )


def solution(mesh):
    placed = (
        P("dp", "ctx", "head", None),
        P("dp", "ctx", "head", None),
        P("dp", "ctx", "head", None),
        P("dp", "ctx", None),
        P("head", None),
        P("head", None, None),
        P("dp", "ctx", "head", None),
    )
    return jax.shard_map(
        local,
        mesh=mesh,
        in_specs=placed,
        out_specs=(
            P("dp", "ctx", "head", None),
            P("dp", "ctx", "head", None),
            P("dp", "ctx", "head", None),
            P("dp", "ctx", None),
            P("head", None),
            P("head", None, None),
        ),
        check_vma=False,
    )
```

profile of v0, /device:TPU:0, one launch (start us, length us, event | category | flops | bytes accessed | tf_op | source)
XLA Modules:
  0.0 373.3 jit_solution(2890952495120564921)
XLA Ops:
  11.0 22.4 %while.117 = (s32[]{:T(128)}, f32[1,6,128,128]{3,2,1,0:T(8,128)S(1)}, f32[1,6,128,128]{3,2,1,0:T(8,128)}, f32[4,1,6,64,128]{4,3,2,1,0:T(8,128)S(1)}, f32[4,1,6,6...) while((s32[]{:T(128)}, f32[1,6,128,128]{3,2,1,0:T(8,128)S(1)}, ...), condition=%wide.region_1.2_spmd.clone, body=%wide.region_0.1_spmd.clone.sunk | while | flops 453574656 | bytes 5911651 | solution.py:87
  35.9 13.1 %while.114 = (s32[]{:T(128)}, f32[4,1,6,64,1]{3,4,2,1,0:T(1,128)}, f32[4,1,6,128,64]{3,4,2,1,0:T(8,128)}, f32[4,1,6,64]{3,0,2,1:T(4,128)}, f32[4,1,6,64,128]{4,3,0,2,1:T(8,128)}, /*index=5*/s32[]{:T(128)}) while((s32[]{:T(128)}, f32[4,1,6,64,1]{3,4,2,1,0:T(1,128)}, f32[4,1,6,128,64]{3,4,2,1,0:T(8,128)}, f32[4,1,6,64]{3,0,2,1:T(4,128)}, ...), condition=%wide.region_3.4_spmd, body=%wide.region_2.3_spmd.sunk | while | flops 2 | bytes 1580105 | solution.py:60
  51.0 23.7 %while.118 = (s32[]{:T(128)}, f32[1,6,128,128]{2,3,1,0:T(8,128)}, f32[4,1,6,64,128]{4,3,2,1,0:T(8,128)S(1)}, f32[4,1,6,64,128]{4,3,2,1,0:T(8,128)}, f32[4,1,6,64...) while((s32[]{:T(128)}, f32[1,6,128,128]{2,3,1,0:T(8,128)}, ...), condition=%wide.region_5.6_spmd.clone, body=%wide.region_4.5_spmd.clone.sunk | while | flops 226934784 | bytes 3155078 | solution.py:60
  82.6 18.8 %all-gather.15.cloned.1.call-done = f32[4,6,128,128]{3,2,1,0:T(8,128)} async-done(((f32[1,6,128,128]{3,2,1,0:T(8,128)}), f32[4,6,128,128]{3,2,1,0:T(8,128)}) %all-gather.15.cloned.1.call-update) | async-done | bytes 1572880 | tf_op jit(solution)/shard_map/all_gather | solution.py:14
  102.3 15.0 %while.120 = (s32[]{:T(128)}, f32[1,6,128,128]{3,2,1,0:T(8,128)S(1)}, f32[1,6,128,128]{3,2,1,0:T(8,128)}, s32[]{:T(128)}, f32[4,1,6,128,128]{4,3,2,1,0:T(8,128)}...) while((s32[]{:T(128)}, f32[1,6,128,128]{3,2,1,0:T(8,128)S(1)}, ...), condition=%wide.region_9.10_spmd.clone, body=%wide.region_8.9_spmd.clone.sunk | while | flops 302481408 | bytes 5114984 | solution.py:26
  103.3 2.4 fusion.232
  108.3 2.4 fusion.232
  113.3 2.4 fusion.232
  118.9 15.9 %all-gather.11.cloned.1.call-done = f32[4,6,128,128]{3,2,1,0:T(8,128)} async-done(((f32[1,6,128,128]{3,2,1,0:T(8,128)}), f32[4,6,128,128]{3,2,1,0:T(8,128)}) %all-gather.11.cloned.1.call-update) | async-done | bytes 1572880 | tf_op jit(solution)/shard_map/all_gather | solution.py:14
  134.8 2.7 reverse_bitcast_fusion
  140.5 23.7 %while.115 = (s32[]{:T(128)}, f32[1,6,128,128]{3,2,1,0:T(8,128)S(1)}, f32[4,1,6,128,128]{4,3,2,1,0:T(8,128)}, f32[4,1,6,64,128]{4,3,2,1,0:T(8,128)}, f32[4,1,6,6...) while((s32[]{:T(128)}, ...), condition=%wide.region_11.12_spmd, body=%wide.region_10.11_spmd.sunk | while | flops 151240704 | bytes 4149369 | solution.py:60
  164.2 3.9 %all-gather.9.cloned.1.call-done = f32[4,6,128,128]{3,2,1,0:T(8,128)} async-done(((f32[1,6,128,128]{3,2,1,0:T(8,128)}), f32[4,6,128,128]{3,2,1,0:T(8,128)}) %all-gather.9.cloned.1.call-update) | async-done | bytes 1572880 | tf_op jit(solution)/shard_map/all_gather | solution.py:14
  168.1 2.7 reverse_bitcast_fusion.1
  170.8 5.2 %while.119 = (s32[]{:T(128)}, f32[1,6,128,128]{3,2,1,0:T(8,128)S(1)}, s32[]{:T(128)}, f32[4,1,6,128,128]{4,3,2,1,0:T(8,128)}, f32[4,1,6,128,128]{4,3,2,1,0:T(8,128)}, /*index=5*/s32[]{:T(128)}, s32[]{:T(128)}) while((s32[]{:T(128)}, f32[1,6,128,128]{3,2,1,0:T(8,128)S(1)}, s32[]{:T(128)}, f32[4,1,6,128,128]{4,3,2,1,0:T(8,128)}, ...), condition=%wide.region_7.8_spmd.clone, body=%wide.region_6.7_spmd.clone.sunk | while | flops 151388160 | bytes 2755167 | solution.py:26
  178.0 50.8 %while.116 = (s32[]{:T(128)}, f32[1,6,128,128]{2,3,1,0:T(8,128)S(1)}, bf16[4,1,6,64,128]{4,3,2,1,0:T(8,128)(2,1)}, bf16[4,1,6,64,128]{4,3,2,1,0:T(8,128)(2,1)}, ...) while((s32[]{:T(128)}, ...), condition=%wide.region_14.15_spmd, body=%wide.region_12.14_spmd.sunk | while | flops 453721728 | bytes 9464565 | solution.py:60
  180.5 2.4 bitcast_dynamic-update-slice_fusion.23
  188.2 2.5 fusion.202
  200.9 2.5 fusion.202
  213.6 2.5 fusion.202
  226.2 2.5 fusion.202
  231.3 2.6 fusion.111
  237.3 102.5 %all-reduce.6.cloned.1.call-done = (f32[6,3072]{1,0:T(8,128)}, f32[6,128,128]{2,1,0:T(8,128)}) async-done(((f32[6,3072]{1,0:T(8,128)}, f32[6,128,128]{2,1,0:T(8,128)}), (f32[6,3072]{1,0:T(8,128)}, f32[6,128,128]{2,1,0:T(8,128)})) %all-reduce.6.cloned.1.call-update) | async-done | bytes 466960 | tf_op jit(solution)/shard_map/psum | solution.py:152
  339.7 22.6 %all-reduce.4.cloned.1.call-done = bf16[1,256,3072]{2,1,0:T(8,128)(2,1)} async-done(((bf16[1,256,3072]{2,1,0:T(8,128)(2,1)}), bf16[1,256,3072]{2,1,0:T(8,128)(2,1)}) %all-reduce.4.cloned.1.call-update) | async-done | bytes 1572880 | tf_op jit(solution)/shard_map/psum | solution.py:154
  362.4 2.7 copy.218
  (250 shorter events, 163.9 us)
Async XLA Ops:
  7.2 75.4 %all-gather.13.cloned.1.call-start = ((), (), s32[]{:S(2)}) async-start(), calls=%async_computation.3 | async-start | bytes 1966080 | tf_op jit(solution)/shard_map/all_gather | solution.py:14
  7.3 3.7 copy-start.11
  34.1 67.3 %all-gather.15.cloned.1.call-start = ((), (), s32[]{:S(2)}) async-start(), calls=%async_computation.4 | async-start | bytes 1966080 | tf_op jit(solution)/shard_map/all_gather | solution.py:14
  34.9 99.9 %all-gather.11.cloned.1.call-start = ((), (), s32[]{:S(2)}) async-start(), calls=%async_computation.2 | async-start | bytes 1966080 | tf_op jit(solution)/shard_map/all_gather | solution.py:14
  35.9 13.1 %copy-start.14 = (bf16[1,256,6,128]{3,1,2,0:T(8,128)(2,1)S(1)}, bf16[1,256,6,128]{3,1,2,0:T(8,128)(2,1)}, u32[]{:S(2)}) copy-start(bf16[1,256,6,128]{3,1,2,0:T(8,128)(2,1)} %param.27) | copy-start | bytes 1179652
  51.0 25.9 %copy-start.2 = (f32[1,6,128,128]{3,2,1,0:T(8,128)S(1)}, f32[1,6,128,128]{3,2,1,0:T(8,128)}, u32[]{:S(2)}) copy-start(f32[1,6,128,128]{3,2,1,0:T(8,128)} %copy-done.1) | copy-start | bytes 1179652
  74.7 6.1 %copy-start.3 = (f32[4,1,6,64,128]{4,3,2,1,0:T(8,128)}, f32[4,1,6,64,128]{4,3,2,1,0:T(8,128)S(1)}, u32[]{:S(2)}) copy-start(f32[4,1,6,64,128]{4,3,2,1,0:T(8,128)S(1)} %get-tuple-element.1699) | copy-start | bytes 2359300
  76.9 91.2 %all-gather.9.cloned.1.call-start = ((), (), s32[]{:S(2)}) async-start(), calls=%async_computation.1 | async-start | bytes 1966080 | tf_op jit(solution)/shard_map/all_gather | solution.py:14
  77.9 261.8 %all-reduce.6.cloned.1.call-start = ((), (), s32[]{:S(2)}) async-start(), calls=%async_computation.5 | async-start | bytes 983040 | tf_op jit(solution)/shard_map/psum | solution.py:152
  170.8 7.1 %copy-start.4 = (f32[4,1,6,64,128]{4,3,2,1,0:T(8,128)S(1)}, f32[4,1,6,64,128]{4,3,2,1,0:T(8,128)}, u32[]{:S(2)}) copy-start(f32[4,1,6,64,128]{4,3,2,1,0:T(8,128)} %copy-done.3) | copy-start | bytes 2359300
  178.0 6.3 %copy-start.7 = (bf16[4,1,6,64,128]{4,3,2,1,0:T(8,128)(2,1)S(1)}, bf16[4,1,6,64,128]{4,3,2,1,0:T(8,128)(2,1)}, u32[]{:S(2)}) copy-start(bf16[4,1,6,64,128]{4,3,2,1,0:T(8,128)(2,1)} %get-tuple-element.1648) | copy-start | bytes 1179652 | tf_op jit(solution)/shard_map/vmap(vmap(transpose(jvp())))/while
  186.2 2.0 copy-start.8
  190.7 6.3 %copy-start.7 = (bf16[4,1,6,64,128]{4,3,2,1,0:T(8,128)(2,1)S(1)}, bf16[4,1,6,64,128]{4,3,2,1,0:T(8,128)(2,1)}, u32[]{:S(2)}) copy-start(bf16[4,1,6,64,128]{4,3,2,1,0:T(8,128)(2,1)} %get-tuple-element.1648) | copy-start | bytes 1179652 | tf_op jit(solution)/shard_map/vmap(vmap(transpose(jvp())))/while
  198.9 2.0 copy-start.8
  203.4 6.3 %copy-start.7 = (bf16[4,1,6,64,128]{4,3,2,1,0:T(8,128)(2,1)S(1)}, bf16[4,1,6,64,128]{4,3,2,1,0:T(8,128)(2,1)}, u32[]{:S(2)}) copy-start(bf16[4,1,6,64,128]{4,3,2,1,0:T(8,128)(2,1)} %get-tuple-element.1648) | copy-start | bytes 1179652 | tf_op jit(solution)/shard_map/vmap(vmap(transpose(jvp())))/while
  211.6 2.0 copy-start.8
  216.1 6.3 %copy-start.7 = (bf16[4,1,6,64,128]{4,3,2,1,0:T(8,128)(2,1)S(1)}, bf16[4,1,6,64,128]{4,3,2,1,0:T(8,128)(2,1)}, u32[]{:S(2)}) copy-start(bf16[4,1,6,64,128]{4,3,2,1,0:T(8,128)(2,1)} %get-tuple-element.1648) | copy-start | bytes 1179652 | tf_op jit(solution)/shard_map/vmap(vmap(transpose(jvp())))/while
  224.2 2.0 copy-start.8
  228.9 2.3 copy-start.17
  231.2 131.2 %all-reduce.4.cloned.1.call-start = ((), (), s32[]{:S(2)}) async-start(), calls=%async_computation | async-start | bytes 3145728 | tf_op jit(solution)/shard_map/psum | solution.py:154
  233.9 1.9 copy-start.9
  233.9 2.6 copy-start.10
  362.4 2.7 copy-start.19
  362.4 3.4 copy-start.12
  (9 other events, 10.6 us)
Sparse Core Ops, SparseCore 0:
  34.3 33.6 all-gather.12
  70.4 30.9 all-gather.14
  103.8 30.9 all-gather.10
  137.1 30.9 all-gather.8
  231.3 108.3 all-reduce.5
  342.6 19.6 all-reduce.3
where the time goes:
time: 376 us; the launch traced here: 373 us
  waiting for transfers between devices  165 us (44%)
  matrix products  121 us (32%)
  local copies, waits for them, and re-layouts  64.7 us (17%)
  between operations  14.4 us (4%)
  other arithmetic  7.17 us (2%)
    psum x1, waiting for transfers between devices, local(): lax.psum((init_term, weight_term), ('dp', 'ctx'))  102 us
    dot_general x61, matrix products, product(): jnp.dot(left, right, precision=lax.Precision.HIGHEST, preferred_element_t...  100 us
    all_gather x4, waiting for transfers between devices, prefix(): pieces = jax.tree.map(lambda part: lax.all_gather(part, axis), value)  38.7 us
    psum x1, waiting for transfers between devices, local(): grad_flat = lax.psum(partial_hidden.astype(jnp.bfloat16), 'head')  22.6 us
    dot_general x10, matrix products, stacked(): jnp.einsum('...ij,...jk->...ik', left, right, precision=lax.Precision.HIG...  18.5 us
    unnamed x50, local copies, waits for them, and re-layouts  17.7 us
    dynamic_update_slice x28, local copies, waits for them, and re-layouts, local_run(): final_state, layer_rows = lax.scan(local_advance, state, blocks)  16.9 us
  transfers between devices with their start and end apart: 6, of which 5 were waited for; matrix products, arithmetic and copies ran while one was open for 27% of the time, Pallas kernels for 0%

commit v1 on v0

v1 whole, which is shorter than its diff:
```python
import functools

import jax
import jax.numpy as jnp
from jax import lax
from jax.experimental import pallas as pl
from jax.experimental.pallas import tpu as pltpu
from jax.sharding import PartitionSpec as P

MINI = 64
RATE_SCALE = 0.5
F32 = jnp.float32
BF16 = jnp.bfloat16
MESH = pl.DeviceIdType.MESH
SPAN = 256


def dot_nn(left, right):
    return jnp.dot(left, right, preferred_element_type=F32)


def dot_tn(left, right):
    return lax.dot_general(left, right, (((0,), (0,)), ((), ())), preferred_element_type=F32)


def dot_nt(left, right):
    return lax.dot_general(left, right, (((1,), (1,)), ((), ())), preferred_element_type=F32)


def b16(value):
    return value.astype(BF16)


def split(value):
    high = b16(value)
    return high, b16(value - high.astype(F32))


def kernel(
    n_dp, n_ctx, n_red, heads, width, toks,
    q_ref, k_ref, v_ref, hid_ref, rw_ref, init_ref, o_ref,
    dq_ref, dk_ref, dv_ref, gh_ref, gw_ref, gi_ref,
    own, lev_send, lev_recv, top_send, top_recv, qo, run_x, run_p, run_res,
    rw_other, dl_send, dl_recv, gi_send, gi_recv, gi_red, gi_all,
    gw_part, gw_recv, gw_red, gw_all,
    lev_ss, lev_rs, top_ss, top_rs, rw_sem, dl_sem,
    gi_ss, gi_rs, gi_as, gi_ar, gw_ss, gw_rs, gw_as, gw_ar,
):
    dp, ctx, head = lax.axis_index("dp"), lax.axis_index("ctx"), lax.axis_index("head")
    levels = n_ctx.bit_length() - 1
    red_ctx = n_red // n_dp
    n_src = n_dp * n_ctx
    me = dp * n_ctx + ctx
    my_red = dp * red_ctx + ctx
    is_red = ctx < red_ctx
    blocks = toks // MINI
    piece_rows = heads * width // n_red
    other_head = {"head": 1 - head}

    barrier = pltpu.get_barrier_semaphore()

    def greet(step, carry):
        peer = lax.rem(me + step, n_src)
        pl.semaphore_signal(
            barrier, inc=1,
            device_id={"dp": peer // n_ctx, "ctx": lax.rem(peer, n_ctx)},
            device_id_type=MESH,
        )
        return carry

    lax.fori_loop(1, n_src, greet, 0)
    pl.semaphore_signal(barrier, inc=1, device_id=other_head, device_id_type=MESH)

    logits = dot_nt(hid_ref[...], rw_ref[...])
    sig = 1.0 / (1.0 + jnp.exp(-logits))
    rates = RATE_SCALE * sig
    slope = RATE_SCALE * sig * (1.0 - sig)
    eye = (
        lax.broadcasted_iota(jnp.int32, (width, width), 0)
        == lax.broadcasted_iota(jnp.int32, (width, width), 1)
    ).astype(F32)
    start = jnp.concatenate([eye, jnp.zeros((width, width), F32)], axis=1)

    def rows(b):
        return slice(b * MINI, (b + 1) * MINI)

    def lanes(h):
        return slice(h * width, (h + 1) * width)

    def rate(b, h):
        return rates[b * MINI : (b + 1) * MINI, h : h + 1]

    def level_copy(level, h):
        partner = jnp.bitwise_xor(ctx, 1 << level)
        return pltpu.make_async_remote_copy(
            src_ref=lev_send.at[level, h], dst_ref=lev_recv.at[level, h],
            send_sem=lev_ss.at[level, h], recv_sem=lev_rs.at[level, h],
            device_id={"ctx": partner}, device_id_type=MESH,
        )

    def top_copy(h):
        partner = jnp.bitwise_xor(ctx, 1 << (levels - 1))
        return pltpu.make_async_remote_copy(
            src_ref=top_send.at[h], dst_ref=top_recv.at[h],
            send_sem=top_ss.at[h], recv_sem=top_rs.at[h],
            device_id={"ctx": partner}, device_id_type=MESH,
        )

    rw_copy = pltpu.make_async_remote_copy(
        src_ref=rw_ref, dst_ref=rw_other, send_sem=rw_sem.at[0], recv_sem=rw_sem.at[1],
        device_id=other_head, device_id_type=MESH,
    )
    dl_copy = pltpu.make_async_remote_copy(
        src_ref=dl_send, dst_ref=dl_recv, send_sem=dl_sem.at[0], recv_sem=dl_sem.at[1],
        device_id=other_head, device_id_type=MESH,
    )

    def local_maps(group):
        fwd = {h: start for h in group}
        back = {h: None for h in group}
        for step in range(blocks):
            b = step
            for h in group:
                key = k_ref[rows(b), lanes(h)]
                val = v_ref[rows(b), lanes(h)].astype(F32)
                if step == 0:
                    res = jnp.concatenate([key.astype(F32), -val], axis=1)
                else:
                    res = dot_nn(key, b16(fwd[h]))
                    res = jnp.concatenate([res[:, :width], res[:, width:] - val], axis=1)
                fwd[h] = fwd[h] - dot_tn(key, b16(rate(b, h) * res))
            b = blocks - 1 - step
            for h in group:
                key = k_ref[rows(b), lanes(h)]
                term = dot_tn(q_ref[rows(b), lanes(h)], o_ref[rows(b), lanes(h)])
                qo[h, b] = term
                total = term if step == 0 else back[h] + term
                back[h] = total - dot_tn(key, b16(rate(b, h) * dot_nn(key, b16(total))))
        for h in group:
            own[h, 0] = fwd[h][:, :width]
            own[h, 1] = fwd[h][:, width:]
            own[h, 2] = back[h]
            lev_send[0, h, 0] = b16(fwd[h][:, :width])
            lev_send[0, h, 1] = b16(fwd[h][:, width:])
            lev_send[0, h, 2] = b16(back[h])

    third = max(heads // 3, 1)
    groups = [list(range(i, min(i + third, heads))) for i in range(0, heads, third)]
    for index, group in enumerate(groups):
        local_maps(group)
        if index == 0:
            pl.semaphore_wait(barrier, n_src)
            rw_copy.start()
        for h in group:
            level_copy(0, h).start()

    prefix, suffix = {}, {}
    comp = {}
    for level in range(levels - 1):
        late = lax.rem(ctx // (1 << level), 2) == 1
        for h in range(heads):
            level_copy(level, h).wait_recv()
            map_in, shift_in, back_in = (lev_recv[level, h, i] for i in range(3))
            if level == 0:
                map_own, shift_own, back_own = (own[h, i] for i in range(3))
                prefix[h] = (
                    jnp.where(late, map_in.astype(F32), eye),
                    jnp.where(late, shift_in.astype(F32), 0.0),
                )
                suffix[h] = (
                    jnp.where(late, eye, map_in.astype(F32)),
                    jnp.where(late, 0.0, back_in.astype(F32)),
                )
            else:
                map_own, shift_own, back_own = comp[h]
                pre_map, pre_shift = prefix[h]
                suf_map, suf_shift = suffix[h]
                prefix[h] = (
                    jnp.where(late, dot_nn(b16(pre_map), map_in), pre_map),
                    jnp.where(late, dot_nn(b16(pre_map), shift_in) + pre_shift, pre_shift),
                )
                suffix[h] = (
                    jnp.where(late, suf_map, dot_nn(map_in, b16(suf_map))),
                    jnp.where(late, suf_shift, dot_tn(b16(suf_map), back_in) + suf_shift),
                )
            early_map = jnp.where(late, map_in, b16(map_own))
            late_map = jnp.where(late, b16(map_own), map_in)
            early_shift = jnp.where(late, shift_in, b16(shift_own))
            late_shift = jnp.where(late, shift_own, shift_in.astype(F32))
            early_back = jnp.where(late, back_in.astype(F32), back_own)
            late_back = jnp.where(late, b16(back_own), back_in)
            both = dot_nn(late_map, jnp.concatenate([early_map, early_shift], axis=1))
            comp[h] = (
                both[:, :width],
                both[:, width:] + late_shift,
                dot_tn(early_map, late_back) + early_back,
            )
            if level < levels - 2:
                for i in range(3):
                    lev_send[level + 1, h, i] = b16(comp[h][i])
                level_copy(level + 1, h).start()
            else:
                upper = ctx // (1 << (levels - 1)) == 1
                middle = dot_nn(b16(comp[h][0]), b16(init_ref[h])) + comp[h][1]
                top_send[h] = b16(jnp.where(upper, comp[h][2], middle))
                top_copy(h).start()

    upper = ctx // (1 << (levels - 1)) == 1
    state, grad = {}, {}
    for h in range(heads):
        top_copy(h).wait_recv()
        got = top_recv[h]
        base = jnp.where(upper, got, b16(init_ref[h]))
        state[h] = dot_nn(b16(prefix[h][0]), base) + prefix[h][1]
        tail = jnp.where(upper, jnp.zeros_like(got), got)
        grad[h] = dot_tn(b16(suffix[h][0]), tail) + suffix[h][1]
        gi_send[h * width : (h + 1) * width] = b16(
            dot_tn(b16(own[h, 0]), b16(grad[h])) + own[h, 2]
        )

    def red_device(r):
        return {"dp": r // red_ctx, "ctx": lax.rem(r, red_ctx)}

    def piece(r):
        return pl.ds(pl.multiple_of(r * piece_rows, piece_rows), piece_rows)

    def not_me(r):
        return jnp.logical_or(r // red_ctx != dp, lax.rem(r, red_ctx) != ctx)

    def gi_copy(r):
        return pltpu.make_async_remote_copy(
            src_ref=gi_send.at[piece(r)], dst_ref=gi_recv.at[dp],
            send_sem=gi_ss.at[r], recv_sem=gi_rs,
            device_id=red_device(r), device_id_type=MESH,
        )

    def for_reds(body):
        def step(r, carry):
            @pl.when(not_me(r))
            def _():
                body(r)
            return carry

        lax.fori_loop(0, n_red, step, 0)

    def for_peers(body):
        def step(i, carry):
            body(lax.rem(me + i, n_src))
            return carry

        lax.fori_loop(1, n_src, step, 0)

    @pl.when(ctx == 0)
    def _():
        for_reds(lambda r: gi_copy(r).start())
        gi_recv[dp] = gi_send[piece(my_red)]

    def all_copy(src, dst, send_sem, recv_sem, peer):
        return pltpu.make_async_remote_copy(
            src_ref=src, dst_ref=dst.at[my_red],
            send_sem=send_sem.at[peer], recv_sem=recv_sem,
            device_id={"dp": peer // n_ctx, "ctx": lax.rem(peer, n_ctx)},
            device_id_type=MESH,
        )

    def drain(ref, sem):
        pltpu.make_async_copy(ref, ref, sem).wait()

    lane = lax.broadcasted_iota(jnp.int32, (MINI, width), 1)
    dl_rows = [jnp.zeros((MINI, width), F32) for _ in range(blocks)]

    def gradients(group):
        for b in range(blocks):
            for h in group:
                key = k_ref[rows(b), lanes(h)]
                val = v_ref[rows(b), lanes(h)].astype(F32)
                now = b16(state[h])
                run_x[h, b] = now
                res = dot_nn(key, now) - val
                run_res[h, b] = res
                step = b16(rate(b, h) * res)
                run_p[h, b] = step
                state[h] = state[h] - dot_tn(key, step)
                dq_ref[rows(b), lanes(h)] = b16(dot_nt(o_ref[rows(b), lanes(h)], b16(state[h])))
        for b in reversed(range(blocks)):
            for h in group:
                key = k_ref[rows(b), lanes(h)]
                total = grad[h] + qo[h, b]
                total16 = b16(total)
                kg = dot_nn(key, total16)
                drate = jnp.sum(kg * run_res[h, b], axis=1, keepdims=True)
                dlogit = -drate * slope[b * MINI : (b + 1) * MINI, h : h + 1]
                dl_rows[b] = jnp.where(lane == h, dlogit, dl_rows[b])
                rkg = rate(b, h) * kg
                rkg16 = b16(rkg)
                dv_ref[rows(b), lanes(h)] = rkg16
                grad[h] = total - dot_tn(key, rkg16)
                left = jnp.concatenate([run_p[h, b], rkg16], axis=1)
                right = jnp.concatenate([total16, run_x[h, b]], axis=1)
                dk_ref[rows(b), lanes(h)] = b16(-dot_nt(left, right))

    half = max(heads // 2, 1)
    gradients(list(range(half)))

    @pl.when(is_red)
    def _():
        @pl.when(ctx == 0)
        def _():
            drain(gi_recv.at[0 : n_dp - 1], gi_rs)

        @pl.when(ctx != 0)
        def _():
            drain(gi_recv.at[0:n_dp], gi_rs)

        gi_red[...] = b16(jnp.sum(gi_recv[...].astype(F32), axis=0))
        for_peers(lambda peer: all_copy(gi_red, gi_all, gi_as, gi_ar, peer).start())
        gi_all[my_red] = gi_red[...]

    gradients(list(range(half, heads)))

    dl_all = jnp.concatenate(dl_rows, axis=0)
    dl_t = jnp.transpose(dl_all)[:8]
    dl_send[...] = dl_t
    dl_copy.start()
    mine = jnp.concatenate(split(dl_t), axis=0)
    features = hid_ref.shape[1]
    gw_part[...] = jnp.zeros_like(gw_part)
    for r in range(features // SPAN):
        both = dot_nn(mine, hid_ref[:, r * SPAN : (r + 1) * SPAN])
        gw_part[r] = both[:8] + both[8:]

    def gw_copy(r):
        return pltpu.make_async_remote_copy(
            src_ref=gw_part.at[r], dst_ref=gw_recv.at[me],
            send_sem=gw_ss.at[r], recv_sem=gw_rs,
            device_id=red_device(r), device_id_type=MESH,
        )

    for_reds(lambda r: gw_copy(r).start())

    rw_copy.wait_recv()
    dl_copy.wait_recv()
    theirs = jnp.concatenate(split(dl_recv[...]), axis=0)
    for r in range(features // SPAN):
        cols = slice(r * SPAN, (r + 1) * SPAN)
        first = b16(dot_tn(mine, rw_ref[:, cols])).astype(F32)
        second = b16(dot_tn(theirs, rw_other[:, cols])).astype(F32)
        gh_ref[:, cols] = b16(first + second)

    @pl.when(is_red)
    def _():
        gw_recv[me] = gw_part[my_red]
        drain(gw_recv.at[0 : n_src - 1], gw_rs)
        gw_red[...] = jnp.sum(gw_recv[...], axis=0)
        for_peers(lambda peer: all_copy(gw_red, gw_all, gw_as, gw_ar, peer).start())
        gw_all[my_red] = gw_red[...]

    def finish(full, sem):
        @pl.when(is_red)
        def _():
            drain(full.at[0 : n_red - 1], sem)

        if n_ctx > red_ctx:
            @pl.when(jnp.logical_not(is_red))
            def _():
                drain(full.at[0:n_red], sem)

    finish(gi_all, gi_ar)
    gi_ref[...] = gi_all[...].astype(F32)
    finish(gw_all, gw_ar)
    gw_ref[...] = gw_all[...]

    for level in range(levels - 1):
        for h in range(heads):
            level_copy(level, h).wait_send()
    for h in range(heads):
        top_copy(h).wait_send()
    rw_copy.wait_send()
    dl_copy.wait_send()

    @pl.when(ctx == 0)
    def _():
        for_reds(lambda r: gi_copy(r).wait_send())

    for_reds(lambda r: gw_copy(r).wait_send())

    @pl.when(is_red)
    def _():
        for_peers(lambda peer: all_copy(gi_red, gi_all, gi_as, gi_ar, peer).wait_send())
        for_peers(lambda peer: all_copy(gw_red, gw_all, gw_as, gw_ar, peer).wait_send())


def local(n_dp, n_ctx, queries, keys, values, hidden_in, rate_weight, state_init, out_grad):
    seqs, toks, heads, width = queries.shape
    features = hidden_in.shape[2]
    n_red = n_dp * min(n_ctx, 4)
    n_src = n_dp * n_ctx
    levels = n_ctx.bit_length() - 1
    blocks = toks // MINI
    gap = jnp.zeros((8 - heads, features), BF16)
    weights = jnp.concatenate([rate_weight, gap, rate_weight, gap], axis=0)
    piece_rows = heads * width // n_red
    flat = (toks, heads * width)
    vmem = pl.BlockSpec(memory_space=pltpu.VMEM)
    dma = pltpu.SemaphoreType.DMA
    scratch = [
        pltpu.VMEM((heads, 3, width, width), F32),
        pltpu.VMEM((levels - 1, heads, 3, width, width), BF16),
        pltpu.VMEM((levels - 1, heads, 3, width, width), BF16),
        pltpu.VMEM((heads, width, width), BF16),
        pltpu.VMEM((heads, width, width), BF16),
        pltpu.VMEM((heads, blocks, width, width), F32),
        pltpu.VMEM((heads, blocks, width, width), BF16),
        pltpu.VMEM((heads, blocks, MINI, width), BF16),
        pltpu.VMEM((heads, blocks, MINI, width), F32),
        pltpu.VMEM((16, features), BF16),
        pltpu.VMEM((8, toks), F32),
        pltpu.VMEM((8, toks), F32),
        pltpu.VMEM((heads * width, width), BF16),
        pltpu.VMEM((n_dp, piece_rows, width), BF16),
        pltpu.VMEM((piece_rows, width), BF16),
        pltpu.VMEM((n_red, piece_rows, width), BF16),
        pltpu.VMEM((n_red, 8, SPAN), F32),
        pltpu.VMEM((n_src, 8, SPAN), F32),
        pltpu.VMEM((8, SPAN), F32),
        pltpu.VMEM((n_red, 8, SPAN), F32),
        dma((levels - 1, heads)), dma((levels - 1, heads)),
        dma((heads,)), dma((heads,)), dma((2,)), dma((2,)),
        dma((n_red,)), dma, dma((n_src,)), dma,
        dma((n_red,)), dma, dma((n_src,)), dma,
    ]
    dq, dk, dv, gh, gw, gi = pl.pallas_call(
        functools.partial(kernel, n_dp, n_ctx, n_red, heads, width, toks),
        out_shape=(
            jax.ShapeDtypeStruct(flat, BF16),
            jax.ShapeDtypeStruct(flat, BF16),
            jax.ShapeDtypeStruct(flat, BF16),
            jax.ShapeDtypeStruct((toks, features), BF16),
            jax.ShapeDtypeStruct((n_red, 8, SPAN), F32),
            jax.ShapeDtypeStruct((n_red, piece_rows, width), F32),
        ),
        in_specs=[vmem] * 7,
        out_specs=[vmem] * 6,
        scratch_shapes=scratch,
        compiler_params=pltpu.CompilerParams(
            collective_id=0, has_side_effects=True, vmem_limit_bytes=56 * 2**20
        ),
    )(
        queries.reshape(flat), keys.reshape(flat), values.reshape(flat),
        hidden_in.reshape(toks, features), weights, state_init, out_grad.reshape(flat),
    )
    grad_rate = jnp.transpose(gw, (1, 0, 2)).reshape(8, n_red * SPAN)[:heads, :features]
    shape = queries.shape
    return (
        dq.reshape(shape), dk.reshape(shape), dv.reshape(shape),
        gh.reshape(hidden_in.shape), grad_rate, gi.reshape(heads, width, width),
    )


def solution(mesh):
    placed = (
        P("dp", "ctx", "head", None),
        P("dp", "ctx", "head", None),
        P("dp", "ctx", "head", None),
        P("dp", "ctx", None),
        P("head", None),
        P("head", None, None),
        P("dp", "ctx", "head", None),
    )
    return jax.shard_map(
        functools.partial(local, mesh.shape["dp"], mesh.shape["ctx"]),
        mesh=mesh,
        in_specs=placed,
        out_specs=(
            P("dp", "ctx", "head", None),
            P("dp", "ctx", "head", None),
            P("dp", "ctx", "head", None),
            P("dp", "ctx", None),
            P("head", None),
            P("head", None, None),
        ),
        check_vma=False,
    )
```

time: 376 us -> 65.3 us (0.17)
  waiting for transfers between devices: 165 us -> 0 us
  matrix products: 121 us -> 0 us
  local copies, waits for them, and re-layouts: 64.7 us -> 12.4 us
  Pallas kernels: 0 us -> 50.3 us
  between operations: 14.4 us -> 0.73 us
  other arithmetic: 7.17 us -> 1.57 us
    psum x2 -> x0, waiting for transfers between devices: 125 us -> none  [the longest x1 102 us: local(): lax.psum((init_term, weight_term), ('dp', 'ctx'))]
    dot_general x73 -> x0, matrix products: 121 us -> none  [the longest x61 100 us: product(): jnp.dot(left, right, precision=lax.Precision.HIGHEST, preferred_element_t...]
    pallas_call x0 -> x1, Pallas kernels: none -> 50.3 us  [local(): pl.pallas_call(functools.partial(kernel, n_dp, n_ctx, n_red, heads, width...]
    all_gather x4 -> x0, waiting for transfers between devices: 38.7 us -> none  [prefix(): pieces = jax.tree.map(lambda part: lax.all_gather(part, axis), value)]
    dynamic_update_slice x28 -> x0, local copies, waits for them, and re-layouts: 16.9 us -> none  [local_run(): final_state, layer_rows = lax.scan(local_advance, state, blocks)]
    while x37 -> x0, local copies, waits for them, and re-layouts: 11.7 us -> none
    unnamed x50 -> x25, local copies, waits for them, and re-layouts: 17.7 us -> 6.51 us
    dynamic_slice x16 -> x0, local copies, waits for them, and re-layouts: 7.29 us -> none  [the longest x8 4.51 us: block_maps(): result, unused = lax.scan(block_advance, start, blocks)]
  transfers between devices with their start and end apart: 6 -> 0, of which waited for: 5 -> 0; matrix products, arithmetic and copies ran while one was open for 27% -> 0% of each run, Pallas kernels for 0% -> 0%
where the time goes in v1:
time: 65.3 us; the launch traced here: 65 us
  Pallas kernels  50.3 us (77%)
  local copies, waits for them, and re-layouts  12.4 us (19%)
  other arithmetic  1.57 us (2%)
  between operations  0.73 us (1%)
    pallas_call x1, Pallas kernels, local(): pl.pallas_call(functools.partial(kernel, n_dp, n_ctx, n_red, heads, width...  50.3 us
    unnamed x25, local copies, waits for them, and re-layouts  6.51 us
    pallas_call x3, local copies, waits for them, and re-layouts, local(): pl.pallas_call(functools.partial(kernel, n_dp, n_ctx, n_red, heads, width...  1.58 us
    concatenate x1, other arithmetic, local(): weights = jnp.concatenate([rate_weight, gap, rate_weight, gap], axis=0)  1.57 us

profile of v1, /device:TPU:0, one launch (start us, length us, event | category | flops | bytes accessed | tf_op | source)
XLA Modules:
  0.0 65.0 jit_solution(11178007372977995735)
XLA Ops:
  0.6 0.0 copy-start.1
  0.7 1.6 %pad_maximum_fusion.rw_ref = bf16[16,3072]{1,0:T(8,128)(2,1)} fusion(bf16[2,3072]{1,0:T(2,128)(2,1)S(1)} %broadcast_in_dim.3, bf16[6,3072]{1,0:T(8,128)(2,1)} %param.11), kind=kLoop, calls=%fused_computation | loop fusion | flops 393216 | bytes 147456 | tf_op jit(solution)/shard_map/concatenate | solution.py:401
  2.2 1.2 %copy.20 = bf16[1,256,6,128]{1,3,2,0:T(8,128)(2,1)S(1)} copy(bf16[1,256,6,128]{3,1,2,0:T(8,128)(2,1)} %param.7) | data formatting | bytes 786432 | tf_op args[0]
  3.5 0.9 %copy.24.q_ref = bf16[256,768]{1,0:T(8,128)(2,1)} copy(bf16[256,768]{0,1:T(8,128)(2,1)S(1)} %bitcast.18) | data formatting | bytes 786432 | tf_op jit(solution)/shard_map/reshape | solution.py:449
  4.4 0.0 copy-done.1
  4.4 0.2 copy.21
  4.6 0.9 %copy.25.k_ref = bf16[256,768]{1,0:T(8,128)(2,1)} copy(bf16[256,768]{0,1:T(8,128)(2,1)S(1)} %bitcast.19) | data formatting | bytes 786432 | tf_op jit(solution)/shard_map/reshape | solution.py:449
  5.5 0.0 copy-done.2
  5.5 0.2 copy.22
  5.7 0.9 %copy.26.v_ref = bf16[256,768]{1,0:T(8,128)(2,1)} copy(bf16[256,768]{0,1:T(8,128)(2,1)S(1)} %bitcast.20) | data formatting | bytes 786432 | tf_op jit(solution)/shard_map/reshape | solution.py:449
  6.6 0.0 copy-done.3
  6.6 0.2 copy.23
  6.8 0.9 %copy.27.o_ref = bf16[256,768]{1,0:T(8,128)(2,1)} copy(bf16[256,768]{0,1:T(8,128)(2,1)S(1)} %bitcast.21) | data formatting | bytes 786432 | tf_op jit(solution)/shard_map/reshape | solution.py:450
  7.7 50.3 %shard_map.118 = (bf16[256,768]{1,0:T(8,128)(2,1)}, bf16[256,768]{1,0:T(8,128)(2,1)}, bf16[256,768]{1,0:T(8,128)(2,1)}, bf16[256,3072]{1,0:T(8,128)(2,1)}, f32[1...) custom-call(bf16[256,768]{1,0:T(8,128)(2,1)} %copy.24.q_ref, bf16[256,768]{1,0:T(8,128)(2,1)} %copy.25.k_ref, ...), custom_call_target="tpu_custom_call" | custom-call | tf_op jit(solution)/shard_map/pallas_call | solution.py:432
  58.0 1.2 %copy.28 = bf16[256,768]{0,1:T(8,128)(2,1)S(1)} copy(bf16[256,768]{1,0:T(8,128)(2,1)} %get-tuple-element.12) | data formatting | bytes 786432 | tf_op jit(solution)/shard_map/pallas_call | solution.py:432
  59.3 0.9 %copy.31 = bf16[1,256,6,128]{3,1,2,0:T(8,128)(2,1)} copy(bf16[1,256,6,128]{1,3,2,0:T(8,128)(2,1)S(1)} %bitcast.15) | data formatting | bytes 786432
  60.2 0.6 slice.4
  60.9 0.2 copy.29
  61.0 0.9 %copy.32 = bf16[1,256,6,128]{3,1,2,0:T(8,128)(2,1)} copy(bf16[1,256,6,128]{1,3,2,0:T(8,128)(2,1)S(1)} %bitcast.16) | data formatting | bytes 786432
  62.0 0.2 copy.30
  62.1 0.9 %copy.33 = bf16[1,256,6,128]{3,1,2,0:T(8,128)(2,1)} copy(bf16[1,256,6,128]{1,3,2,0:T(8,128)(2,1)S(1)} %bitcast.17) | data formatting | bytes 786432
  63.1 1.1 %copy.36 = bf16[1,256,3072]{2,1,0:T(8,128)(2,1)} copy(bf16[1,256,3072]{2,1,0:T(8,128)(2,1)S(1)} %bitcast.14) | data formatting | bytes 3145728
  64.2 0.1 copy-done.4
  64.3 0.7 %copy.37 = f32[6,128,128]{2,1,0:T(8,128)} copy(f32[6,128,128]{2,1,0:T(8,128)S(1)} %bitcast.22) | data formatting | bytes 786432
  (12 shorter events, 0.0 us)
Async XLA Ops:
  0.6 3.7 %copy-start.1 = (bf16[1,256,6,128]{3,1,2,0:T(8,128)(2,1)S(1)}, bf16[1,256,6,128]{3,1,2,0:T(8,128)(2,1)}, u32[]{:S(2)}) copy-start(bf16[1,256,6,128]{3,1,2,0:T(8,128)(2,1)} %param.8) | copy-start | bytes 1179652
  2.2 3.3 %copy-start.2 = (bf16[1,256,6,128]{3,1,2,0:T(8,128)(2,1)S(1)}, bf16[1,256,6,128]{3,1,2,0:T(8,128)(2,1)}, u32[]{:S(2)}) copy-start(bf16[1,256,6,128]{3,1,2,0:T(8,128)(2,1)} %param.9) | copy-start | bytes 1179652
  4.4 2.2 %copy-start.3 = (bf16[1,256,6,128]{3,1,2,0:T(8,128)(2,1)S(1)}, bf16[1,256,6,128]{3,1,2,0:T(8,128)(2,1)}, u32[]{:S(2)}) copy-start(bf16[1,256,6,128]{3,1,2,0:T(8,128)(2,1)} %param.13) | copy-start | bytes 1179652
  58.0 2.2 %copy-start.7 = (f32[16,8,256]{2,1,0:T(8,128)S(1)}, f32[16,8,256]{2,1,0:T(8,128)}, u32[]{:S(2)}) copy-start(f32[16,8,256]{2,1,0:T(8,128)} %get-tuple-element.16) | copy-start | bytes 393220
  58.0 2.8 %copy-start.6 = (bf16[256,768]{1,0:T(8,128)(2,1)S(1)}, bf16[256,768]{1,0:T(8,128)(2,1)}, u32[]{:S(2)}) copy-start(bf16[256,768]{1,0:T(8,128)(2,1)} %get-tuple-element.13) | copy-start | bytes 1179652
  58.0 3.9 %copy-start.5 = (bf16[256,768]{1,0:T(8,128)(2,1)S(1)}, bf16[256,768]{1,0:T(8,128)(2,1)}, u32[]{:S(2)}) copy-start(bf16[256,768]{1,0:T(8,128)(2,1)} %get-tuple-element.14) | copy-start | bytes 1179652
  60.9 2.2 %copy-start = (bf16[256,3072]{1,0:T(8,128)(2,1)S(1)}, bf16[256,3072]{1,0:T(8,128)(2,1)}, u32[]{:S(2)}) copy-start(bf16[256,3072]{1,0:T(8,128)(2,1)} %get-tuple-element.15) | copy-start | bytes 4718596
  63.1 1.2 %copy-start.4 = (f32[16,48,128]{2,1,0:T(8,128)S(1)}, f32[16,48,128]{2,1,0:T(8,128)}, u32[]{:S(2)}) copy-start(f32[16,48,128]{2,1,0:T(8,128)} %get-tuple-element.17) | copy-start | bytes 1179652
